TPU v7x, 128 devices: a whole 4x4x4 slice. The times are simulated.
128 devices in a mesh: rows: 16 (over z, x_hi, core), cols: 8 (over x_lo, y).
Axes of the slice: x: 4 (x_hi: 2, x_lo: 2; x = x_hi * 2 + x_lo), y: 4, z: 4, core: 2. Of those that a mesh axis runs over, the one named last changes fastest.
Arguments:
- slm_field: float32 [2, 4096, 2048], P(None, 'rows', 'cols'), may hold values from -6 to 6
- target_light: float32 [32, 16, 256], P('rows', 'cols'), may hold values from 0 to 0.5
Outputs:
- gradient: float32 [2, 4096, 2048], P(None, 'rows', 'cols')
- light_field: float32 [32, 16, 256], P('rows', 'cols')
All inputs are finite; a program needn't handle non-finite values.
Results may differ from a plain program's by a relative error of at most 0.012.
Values may be sent and summed in bfloat16 or wider, within the bound.
A program may use at most 64 MiB of HBM per device.

v0:
```python
import functools
import math

import jax
import jax.numpy as jnp
import numpy as np
from jax import lax
from jax.experimental import pallas as pl
from jax.experimental.pallas import tpu as pltpu
from jax.sharding import PartitionSpec as P

MESH = pl.DeviceIdType.MESH

f32, bf16 = jnp.float32, jnp.bfloat16

def mm(a, b, dims=((1,), (0,))):
    return lax.dot_general(a, b, (dims, ((), ())), preferred_element_type=f32)

def roll(x, shift):
    return pltpu.roll(x, shift, x.ndim - 1)

def turn(pair, angle):
    re, im = pair
    c, s = math.cos(angle), math.sin(angle)
    if abs(s) < 1e-9:
        return (re, im) if c > 0 else (-re, -im)
    if abs(c) < 1e-9:
        return (-im, re) if s > 0 else (im, -re)
    if abs(abs(c) - abs(s)) < 1e-9:
        k = abs(c)
        a, b = (re, im) if c > 0 else (-re, -im)
        if (s > 0) == (c > 0):
            return k * (a - b), k * (a + b)
        return k * (a + b), k * (b - a)
    return re * c - im * s, re * s + im * c

def fft_list(xs, sign):
    n = len(xs)
    if n == 1:
        return list(xs)
    even, odd = fft_list(xs[0::2], sign), fft_list(xs[1::2], sign)
    out = [None] * n
    for k in range(n // 2):
        t = turn(odd[k], sign * 2 * math.pi * k / n)
        e = even[k]
        out[k] = (e[0] + t[0], e[1] + t[1])
        out[k + n // 2] = (e[0] - t[0], e[1] - t[1])
    return out

def real_fft8(x):
    s = math.sqrt(0.5)
    a0, a1 = x[0] + x[4], x[0] - x[4]
    b0, b1 = x[2] + x[6], x[2] - x[6]
    c0, c1 = x[1] + x[5], x[1] - x[5]
    d0, d1 = x[3] + x[7], x[3] - x[7]
    e1, f1 = s * (c1 - d1), s * (c1 + d1)
    r1, r3 = a1 + e1, a1 - e1
    i1, i3 = -(b1 + f1), b1 - f1
    r2, i2 = a0 - b0, d0 - c0
    p, q = a0 + b0, c0 + d0
    return [(p + q, None), (r1, i1), (r2, i2), (r3, i3), (p - q, None), (r3, -i3), (r2, -i2), (r1, -i1)]

def lane_swap(xs):
    lane = lax.broadcasted_iota(jnp.int32, xs[0].shape, xs[0].ndim - 1)
    for step, (pairs, width) in enumerate((( ((0, 1), (2, 3)), 32), (((0, 2), (1, 3)), 64))):
        low = (lane // width) % 2 == 0
        out = [None] * 4
        for lo, hi in pairs:
            out[lo] = jnp.where(low, xs[lo], roll(xs[hi], width))
            out[hi] = jnp.where(low, roll(xs[lo], 128 - width), xs[hi])
        xs = out
    return xs

def by_i(x):
    lane = lax.broadcasted_iota(jnp.int32, x.shape, x.ndim - 1)
    return jnp.where(lane < 64, -1.0, 1.0) * roll(x, 64)

def tables():
    a = np.arange(256)
    t256 = 2 * np.pi * ((a[:, None] * a[None]) % 256) / 256
    C, S = np.cos(t256), np.sin(t256)
    cs = np.concatenate([C, S], 1)
    b = np.arange(128)
    t128 = 2 * np.pi * ((b[:, None] * b[None]) % 128) / 128
    c1, s1 = np.cos(t128), np.sin(t128)
    dfwd = np.block([[c1, -s1], [s1, c1]])
    dinv = np.block([[c1, s1], [-s1, c1]])
    taper = np.sin(np.pi * (a + 0.5) / 256) ** 2
    tr = taper[:, None] * C
    ti = -taper[:, None] * S
    rr, rim = tr / 256, ti / 256
    row = np.zeros((2, 256, 4, 2, 64))
    for g in range(4):
        s = slice(64 * g, 64 * g + 64)
        row[0, :, g, 0], row[0, :, g, 1] = rr[:, s], rim[:, s]
        row[1, :, g, 0], row[1, :, g, 1] = -rim[:, s], rr[:, s]
    row = row.reshape(512, 512)
    ct = np.concatenate([tr.T, ti.T], 1)
    cth = np.concatenate([tr, ti], 1)
    v0 = np.arange(8)
    th = 2 * np.pi * v0[:, None] * a[None] / 2048
    u0 = np.arange(32)
    t4 = 2 * np.pi * u0[:, None] * b[None] / 4096
    l = np.arange(128)
    ones = ((l[:, None] % 64) // 16 == (l[None] % 64) // 16) / 256.0
    B = lambda x: x.astype(jnp.bfloat16)
    F = lambda x: x.astype(np.float32)
    return dict(cs=B(cs), dfwd=B(dfwd), dinv=B(dinv), row=B(row), rowh=B(row.T.copy()), ct=B(ct), cth=B(cth),
                tw=F(np.stack([np.cos(th), np.sin(th)])),
                twl=F(np.broadcast_to(np.stack([np.cos(th), np.sin(th)])[..., None], (2, 8, 256, 128))),
                t4=F(np.stack([np.cos(t4), np.sin(t4)])), ones=B(ones))

def filt(me):
    q, k = me // 32, me % 32
    u0 = lax.broadcasted_iota(jnp.int32, (32, 16, 128), 0)
    w = lax.broadcasted_iota(jnp.int32, (32, 16, 128), 1)
    u1 = lax.broadcasted_iota(jnp.int32, (32, 16, 128), 2)
    u = 32 * u1 + u0
    v = 8 * (8 * k + w % 8) + 2 * q + w // 8
    fx = jnp.where(u < 2048, u, u - 4096).astype(f32) / 4096
    fy = jnp.where(v < 1024, v, v - 2048).astype(f32) / 2048
    s = fx * fx + fy * fy
    turns = 16000.0 * s / (jnp.sqrt(225.0 - s) + 15.0)
    quarters = 4.0 * (turns - jnp.floor(turns))
    nearest = jnp.floor(quarters + 0.5)
    z = (quarters - nearest) * (math.pi / 2)
    n = nearest.astype(jnp.int32)
    zz = z * z
    sine = z * (1 + zz * (-1 / 6 + zz * (1 / 120 + zz * (-1 / 5040 + zz / 362880))))
    cosine = 1 + zz * (-1 / 2 + zz * (1 / 24 + zz * (-1 / 720 + zz / 40320)))
    odd = n % 2 == 1
    c, d = jnp.where(odd, sine, cosine), jnp.where(odd, cosine, sine)
    half = 2.0 ** -23
    c = jnp.where((n % 4 == 1) | (n % 4 == 2), -half, half) * c
    d = jnp.where(n % 4 >= 2, half, -half) * d
    return c.reshape(512, 128), d.reshape(512, 128)

def stage_a(x, T):
    z = fft_list([(x[c, 0], x[c, 1]) for c in range(8)], -1)
    rows = []
    zz = []
    for v in range(8):
        c, s = T["tw"][0, v:v + 1], T["tw"][1, v:v + 1]
        re, im = z[v]
        zz.append((re * c + im * s, im * c - re * s) if v else (re, im))
    for q in range(4):
        for v in (2 * q, 2 * q + 1):
            rows.append(jnp.concatenate([zz[v][0], zz[v][1]], 1).astype(bf16))
        for v in (2 * q, 2 * q + 1):
            rows.append(jnp.concatenate([zz[v][1], -zz[v][0]], 1).astype(bf16))
    y = mm(T["cs"][...], jnp.concatenate(rows, 0), ((1,), (1,)))
    return [y[:, 128 * q:128 * q + 128].reshape(32, 8, 128) for q in range(4)]

def columns(xs, T, kr, ki, sign):
    z = fft_list(xs, -1)
    lhs = []
    for u in range(32):
        c, s = T["t4"][0, u:u + 1], T["t4"][1, u:u + 1]
        re, im = z[u]
        lhs.append(jnp.concatenate([re * c + im * s, im * c - re * s], 1).astype(bf16))
    f = mm(jnp.concatenate(lhs, 0), T["dfwd"][...])
    fr, fi = f[:, :128], f[:, 128:]
    if sign > 0:
        pr, pi = fr * kr - fi * ki, fr * ki + fi * kr
    else:
        pr, pi = fr * kr + fi * ki, fi * kr - fr * ki
    g = mm(jnp.concatenate([pr, pi], 1).astype(bf16), T["dinv"][...])
    ys = []
    for u in range(32):
        c, s = T["t4"][0, u:u + 1], T["t4"][1, u:u + 1]
        re, im = g[16 * u:16 * u + 16, :128], g[16 * u:16 * u + 16, 128:]
        ys.append((re * c - im * s, im * c + re * s))
    return fft_list(ys, 1)

def stage_b(r2, T, kr, ki):
    b = lane_swap([r2[:, g] for g in range(4)])
    xs = [(jnp.concatenate([b[0][i], b[1][i]], 0), jnp.concatenate([b[2][i], b[3][i]], 0)) for i in range(32)]
    n = columns(xs, T, kr, ki, 1)
    n = [(re.astype(bf16), im.astype(bf16)) for re, im in n]
    lhs = jnp.concatenate([jnp.concatenate([n[i][0], n[(i + 1) % 32][0], n[i][1], n[(i + 1) % 32][1]], 1) for i in range(32)], 0)
    o = mm(lhs, T["row"][...])
    return [o[:, 128 * g:128 * g + 128].reshape(32, 16, 128).astype(bf16) for g in range(4)]

def stage_c(r3, target, T):
    x = r3.astype(f32).reshape(4, 32, 2, 8, 128)
    cols = []
    for v in range(8):
        xv = x[v // 2, :, v % 2].reshape(256, 128)
        cols.append(jnp.concatenate([xv.astype(bf16), by_i(xv).astype(bf16)], 0))
    o = mm(T["cs"][...], jnp.concatenate(cols, 1))
    ps = []
    for v in range(8):
        zv = o[:, 128 * v:128 * v + 128]
        ps.append((zv * T["twl"][0, v], zv * T["twl"][1, v]))
    near = [p + by_i(q) for p, q in fft_list(ps, 1)]
    nb = [n.astype(bf16) for n in near]
    jb = [by_i(n).astype(bf16) for n in near]
    spec = []
    for j in range(16):
        c, d = j // 2, (j // 2 + 1) % 8
        if j % 2 == 0:
            rhs = jnp.concatenate([nb[c], jb[c]], 0)
        else:
            rhs = jnp.concatenate([nb[c][128:], nb[d][:128], jb[c][128:], jb[d][:128]], 0)
        spec.append(mm(T["ct"][...], rhs))
    sums = jnp.concatenate([(s * s).reshape(16, 16, 128).sum(1) for s in spec], 0)
    hi = sums.astype(bf16)
    lo = (sums - hi.astype(f32)).astype(bf16)
    light = mm(hi, T["ones"][...]) + mm(lo, T["ones"][...])
    wt = 4.0 * (light - target)
    back = []
    for j in range(16):
        w = spec[j] * jnp.concatenate([jnp.broadcast_to(wt[r:r + 1], (16, 128)) for r in range(16 * j, 16 * j + 16)], 0)
        back.append(mm(T["cth"][...], jnp.concatenate([w.astype(bf16), (-by_i(w)).astype(bf16)], 0)))
    bn = []
    for c in range(8):
        e, o_, l = back[2 * c], back[2 * c + 1], back[(2 * c - 1) % 16]
        bn.append(jnp.concatenate([e[:128] + l[128:], o_[:128] + e[128:]], 0))
    cols = []
    for v, (e, f) in enumerate(real_fft8(bn)):
        c, s = T["twl"][0, v], T["twl"][1, v]
        if f is None:
            p, q = e * c, -e * s
        else:
            p, q = e * c + f * s, f * c - e * s
        h = p + by_i(q)
        cols.append(jnp.concatenate([h.astype(bf16), (-by_i(h)).astype(bf16)], 0))
    y = mm(T["cs"][...], jnp.concatenate(cols, 1))
    outs = []
    for q in range(4):
        a = y[:, 256 * q:256 * q + 128].reshape(32, 1, 8, 128)
        b = y[:, 256 * q + 128:256 * q + 256].reshape(32, 1, 8, 128)
        outs.append(jnp.concatenate([a, b], 1).reshape(32, 16, 128).astype(bf16))
    return outs, light

def stage_d(r4, T, kr, ki):
    lhs = jnp.concatenate([r4[:, g].reshape(512, 128) for g in range(4)], 1)
    o = mm(lhs, T["rowh"][...])
    xs = []
    for i in range(32):
        a, b = o[16 * i:16 * i + 16], o[16 * ((i - 1) % 32):16 * ((i - 1) % 32) + 16]
        xs.append((a[:, :128] + b[:, 128:256], a[:, 256:384] + b[:, 384:]))
    n = columns(xs, T, kr, ki, -1)
    parts = []
    for ri in range(2):
        for v in range(2):
            parts.append(jnp.stack([n[i][ri][8 * v:8 * v + 8] for i in range(32)], 0))
    return lane_swap(parts)

def stage_e(r5, T):
    x = jnp.concatenate([r5[q].reshape(256, 128).T for q in range(4)], 0).astype(bf16)
    o = mm(x, T["cs"][...])
    zs = []
    for v in range(8):
        b = 128 * (v // 2) + 32 * (v % 2)
        pr, pi = o[b:b + 32], o[b + 64:b + 96]
        re, im = pr[:, :256] - pi[:, 256:], pi[:, :256] + pr[:, 256:]
        if v:
            c, s = T["tw"][0, v:v + 1], T["tw"][1, v:v + 1]
            re, im = re * c - im * s, im * c + re * s
        zs.append((re, im))
    return fft_list(zs, 1)


NAMES = ("cs", "dfwd", "dinv", "row", "rowh", "ct", "cth", "tw", "twl", "t4", "ones", "spread", "pick")


def exact(x, table):
    hi = x.astype(bf16)
    rest = x - hi.astype(f32)
    mid = rest.astype(bf16)
    low = (rest - mid.astype(f32)).astype(bf16)
    return mm(hi, table) + mm(mid, table) + mm(low, table)


def body(field, target, *refs):
    n = len(NAMES)
    hbm, refs = dict(zip(NAMES, refs[:n])), refs[n:]
    grad, light_out = refs[:2]
    T, refs = dict(zip(NAMES, refs[2:2 + n])), refs[2 + n:]
    x1, r1, ts, tr, s2, r2, s3, r3, ls, lr, s4, r4, s5, r5, s6, r6, kr, ki, tsem, ssem, rsem = refs
    row, col = lax.axis_index("rows"), lax.axis_index("cols")
    me = row * 8 + col

    def place(d):
        return (d // 8, lax.rem(d, 8))

    loads = [pltpu.make_async_copy(hbm[k], T[k], tsem.at[i]) for i, k in enumerate(NAMES)]
    for copy in loads:
        copy.start()
    barrier = pltpu.get_barrier_semaphore()

    def greet(k, _):
        pl.semaphore_signal(barrier, inc=1, device_id=place(lax.rem(me + k, 128)), device_id_type=MESH)
        return 0

    lax.fori_loop(1, 128, greet, 0)

    def copy_to(src, dst, slot, d):
        return pltpu.make_async_remote_copy(src, dst, ssem.at[slot], rsem.at[slot], device_id=d, device_id_type=MESH)

    def send_cols(src, dst, slot):
        for k in range(1, 8):
            d = lax.rem(col + k, 8)
            copy_to(src.at[d], dst.at[col], slot, (row, d)).start()
        dst[pl.ds(col, 1)] = src[pl.ds(col, 1)]

    def send_all(src, dst, slot):
        def one(k, _):
            d = lax.rem(me + k, 128)
            copy_to(src.at[d], dst.at[me], slot, place(d)).start()
            return 0

        lax.fori_loop(1, 128, one, 0)
        dst[pl.ds(me, 1)] = src[pl.ds(me, 1)]

    def arrived(dst, slot):
        some = dst.at[pl.ds(0, dst.shape[0] - 1)]
        copy_to(some, some, slot, (row, col)).wait_recv()

    def sent(src, slot):
        some = src.at[pl.ds(0, src.shape[0] - 1)]
        copy_to(some, some, slot, (row, col)).wait_send()

    for c in range(8):
        x1[c] = field[:, 32 * c:32 * c + 32, :].astype(bf16)
    for copy in loads:
        copy.wait()
    lane = lax.broadcasted_iota(jnp.int32, (4, 16, 256), 2) % 16
    which = lax.broadcasted_iota(jnp.int32, (4, 16, 256), 1)
    chosen = jnp.where(lane == which, jnp.broadcast_to(target[...][:, None, :], (4, 16, 256)), 0.0)
    goals = exact(chosen.reshape(64, 256), T["spread"][...])
    for i in range(2):
        for g in range(4):
            ts[4 * i + g] = goals[32 * i:32 * i + 32, 128 * g:128 * g + 128]
    pl.semaphore_wait(barrier, 127)
    send_cols(x1, r1, 0)
    send_cols(ts, tr, 1)
    a, b = filt(me)
    kr[...] = a
    ki[...] = b
    arrived(r1, 0)
    for q, y in enumerate(stage_a(r1[...].astype(f32), T)):
        s2[32 * q:32 * q + 32] = y
    send_all(s2, r2, 2)
    arrived(r2, 2)
    for g, y in enumerate(stage_b(r2[...].reshape(32, 4, 8, 128), T, kr[...], ki[...])):
        for i in range(32):
            s3[4 * i + g] = y[i]
    send_all(s3, r3, 3)
    arrived(tr, 1)
    arrived(r3, 3)
    ys, light = stage_c(r3[...], tr[...].reshape(256, 128), T)
    for q, y in enumerate(ys):
        s4[32 * q:32 * q + 32] = y
    send_all(s4, r4, 4)
    ls[...] = light.reshape(8, 32, 128)
    send_cols(ls, lr, 5)
    arrived(r4, 4)
    for g, y in enumerate(stage_d(r4[...].reshape(32, 4, 16, 128), T, kr[...], ki[...])):
        for i in range(32):
            s5[4 * i + g] = y[i]
    send_all(s5, r5, 6)
    arrived(lr, 5)
    parts = [jnp.concatenate([lr[4 * i + g] for g in range(4)], 1) for i in range(2)]
    picked = exact(jnp.concatenate(parts, 0), T["pick"][...]).reshape(4, 16, 256)
    light_out[...] = jnp.where(lane == which, picked, 0.0).sum(1)
    arrived(r5, 6)
    for c, (re, im) in enumerate(stage_e(r5[...].reshape(4, 32, 8, 128), T)):
        s6[c, 0] = re.astype(bf16)
        s6[c, 1] = im.astype(bf16)
    send_cols(s6, r6, 7)
    arrived(r6, 7)
    for c in range(8):
        grad[:, 32 * c:32 * c + 32, :] = r6[c].astype(f32)
    for slot, src in enumerate((x1, ts, s2, s3, s4, ls, s5, s6)):
        sent(src, slot)


def local(slm_field, target_light):
    T = tables()
    a = np.arange(256) // 16
    lanes = np.arange(512)
    view = 4 * (lanes // 128) + (lanes % 64) // 16
    spread = a[:, None] == view[None]
    T["spread"] = spread.astype(jnp.bfloat16)
    T["pick"] = (spread & (lanes % 128 % 16 == 0) & (lanes % 128 < 64)).T.astype(jnp.bfloat16)
    consts = [jnp.asarray(T[k]) for k in NAMES]
    vmem, anywhere = pl.BlockSpec(memory_space=pltpu.VMEM), pl.BlockSpec(memory_space=pl.ANY)
    V = pltpu.VMEM
    wide, f_all, b_all = V((8, 2, 32, 256), bf16), V((128, 8, 128), f32), V((128, 16, 128), bf16)
    small = V((8, 32, 128), f32)
    gradient, light = pl.pallas_call(
        body,
        out_shape=(jax.ShapeDtypeStruct((2, 256, 256), f32), jax.ShapeDtypeStruct((4, 256), f32)),
        in_specs=[vmem, vmem] + [anywhere] * len(NAMES),
        out_specs=(vmem, vmem),
        scratch_shapes=[V(T[k].shape, T[k].dtype) for k in NAMES]
        + [wide, wide, small, small, f_all, f_all, b_all, b_all, small, small, b_all, b_all, f_all, f_all, wide, wide]
        + [V((512, 128), f32)] * 2
        + [pltpu.SemaphoreType.DMA((len(NAMES),)), pltpu.SemaphoreType.DMA((8,)), pltpu.SemaphoreType.DMA((8,))],
        compiler_params=pltpu.CompilerParams(collective_id=0, has_side_effects=True, vmem_limit_bytes=56 << 20),
    )(slm_field, target_light.reshape(4, 256), *consts)
    return gradient, light.reshape(2, 2, 256)


def solution(mesh):
    return jax.shard_map(
        local,
        mesh=mesh,
        in_specs=(P(None, "rows", "cols"), P("rows", "cols", None)),
        out_specs=(P(None, "rows", "cols"), P("rows", "cols", None)),
        check_vma=False,
    )
```

profile of v0, /device:TPU:1, one launch (start us, length us, event | category | flops | bytes accessed | tf_op | source)
XLA Modules:
  0.0 76.2 jit_solution(10344476972753828150)
XLA Ops:
  0.6 1.3 %reshape.10.target = f32[4,256]{1,0:T(4,128)} reshape(f32[2,2,256]{2,1,0:T(2,128)} %param.16) | data formatting | bytes 8192 | tf_op jit(solution)/shard_map/reshape | solution.py:403
  1.9 71.2 %shard_map.158 = (f32[2,256,256]{2,1,0:T(8,128)}, f32[4,256]{1,0:T(4,128)}) custom-call(f32[2,256,256]{2,1,0:T(8,128)} %field.1, f32[4,256]{1,0:T(4,128)} %reshape.10.target, bf16[256,512]{1,0:T(8,128)(2,1)} %constant.26.clone.refs_0_, bf16[256,256]{1,0:T(8,128)(2,1)} %constant.27.clone.refs_1_, bf16[256,256]{1,0:T(8,128)(2,1)} %constant.28.clone.refs_2_, ...), custom_call_target="tpu_custom_call" | custom-call | tf_op jit(solution)/shard_map/pallas_call | solution.py:393
  73.1 1.3 %reshape.11 = f32[2,2,256]{2,1,0:T(2,128)} reshape(f32[4,256]{1,0:T(4,128)} %get-tuple-element.5) | data formatting | bytes 8192 | tf_op jit(solution)/shard_map/reshape | solution.py:404
  74.4 1.9 %copy.18 = f32[2,256,256]{2,1,0:T(8,128)} copy(f32[2,256,256]{2,1,0:T(8,128)} %get-tuple-element.8) | data formatting | bytes 1048576
where the time goes:
time: 76.5 us; the launch traced here: 76.2 us
  Pallas kernels  71.2 us (93%)
  local copies, waits for them, and re-layouts  4.44 us (6%)
    pallas_call x1, Pallas kernels, local(): pl.pallas_call(body, out_shape=(jax.ShapeDtypeStruct((2, 256, 256), f32),...  71.2 us
    unnamed x1, local copies, waits for them, and re-layouts  1.87 us

commit v1 on v0

--- a/solution.py
+++ b/solution.py
@@ -276,9 +276,9 @@
 def body(field, target, *refs):
     n = len(NAMES)
     hbm, refs = dict(zip(NAMES, refs[:n])), refs[n:]
-    grad, light_out = refs[:2]
+    r6, light_out = refs[:2]
     T, refs = dict(zip(NAMES, refs[2:2 + n])), refs[2 + n:]
-    x1, r1, ts, tr, s2, r2, s3, r3, ls, lr, s4, r4, s5, r5, s6, r6, kr, ki, tsem, ssem, rsem = refs
+    x1, r1, ts, tr, s2, r2, s3, r3, ls, lr, s4, r4, s5, r5, s6, kr, ki, tsem, ssem, rsem = refs
     row, col = lax.axis_index("rows"), lax.axis_index("cols")
     me = row * 8 + col
 
@@ -286,15 +286,15 @@
         return (d // 8, lax.rem(d, 8))
 
     loads = [pltpu.make_async_copy(hbm[k], T[k], tsem.at[i]) for i, k in enumerate(NAMES)]
+    barrier = pltpu.get_barrier_semaphore()
+
+    for k in range(1, 8):
+        pl.semaphore_signal(barrier, inc=1, device_id=(row, lax.rem(col + k, 8)), device_id_type=MESH)
+    for k in range(1, 16):
+        pl.semaphore_signal(barrier, inc=1, device_id=(lax.rem(row + k, 16), col), device_id_type=MESH)
+
     for copy in loads:
         copy.start()
-    barrier = pltpu.get_barrier_semaphore()
-
-    def greet(k, _):
-        pl.semaphore_signal(barrier, inc=1, device_id=place(lax.rem(me + k, 128)), device_id_type=MESH)
-        return 0
-
-    lax.fori_loop(1, 128, greet, 0)
 
     def copy_to(src, dst, slot, d):
         return pltpu.make_async_remote_copy(src, dst, ssem.at[slot], rsem.at[slot], device_id=d, device_id_type=MESH)
@@ -303,7 +303,12 @@
         for k in range(1, 8):
             d = lax.rem(col + k, 8)
             copy_to(src.at[d], dst.at[col], slot, (row, d)).start()
-        dst[pl.ds(col, 1)] = src[pl.ds(col, 1)]
+        if dst is r6:
+            own = pltpu.make_async_copy(src.at[col], dst.at[col], tsem.at[0])
+            own.start()
+            own.wait()
+        else:
+            dst[pl.ds(col, 1)] = src[pl.ds(col, 1)]
 
     def send_all(src, dst, slot):
         def one(k, _):
@@ -328,12 +333,13 @@
         copy.wait()
     lane = lax.broadcasted_iota(jnp.int32, (4, 16, 256), 2) % 16
     which = lax.broadcasted_iota(jnp.int32, (4, 16, 256), 1)
-    chosen = jnp.where(lane == which, jnp.broadcast_to(target[...][:, None, :], (4, 16, 256)), 0.0)
-    goals = exact(chosen.reshape(64, 256), T["spread"][...])
+    rows = [jnp.broadcast_to(target[i, j:j + 1], (16, 256)) for i in range(2) for j in range(2)]
+    chosen = jnp.where((lane == which).reshape(64, 256), jnp.concatenate(rows, 0), 0.0)
+    goals = exact(chosen, T["spread"][...])
     for i in range(2):
         for g in range(4):
             ts[4 * i + g] = goals[32 * i:32 * i + 32, 128 * g:128 * g + 128]
-    pl.semaphore_wait(barrier, 127)
+    pl.semaphore_wait(barrier, 22)
     send_cols(x1, r1, 0)
     send_cols(ts, tr, 1)
     a, b = filt(me)
@@ -341,10 +347,10 @@
     ki[...] = b
     arrived(r1, 0)
     for q, y in enumerate(stage_a(r1[...].astype(f32), T)):
-        s2[32 * q:32 * q + 32] = y
+        s2[32 * q:32 * q + 32] = y.astype(bf16)
     send_all(s2, r2, 2)
     arrived(r2, 2)
-    for g, y in enumerate(stage_b(r2[...].reshape(32, 4, 8, 128), T, kr[...], ki[...])):
+    for g, y in enumerate(stage_b(r2[...].astype(f32).reshape(32, 4, 8, 128), T, kr[...], ki[...])):
         for i in range(32):
             s3[4 * i + g] = y[i]
     send_all(s3, r3, 3)
@@ -359,22 +365,27 @@
     arrived(r4, 4)
     for g, y in enumerate(stage_d(r4[...].reshape(32, 4, 16, 128), T, kr[...], ki[...])):
         for i in range(32):
-            s5[4 * i + g] = y[i]
+            s5[4 * i + g] = y[i].astype(bf16)
     send_all(s5, r5, 6)
     arrived(lr, 5)
     parts = [jnp.concatenate([lr[4 * i + g] for g in range(4)], 1) for i in range(2)]
     picked = exact(jnp.concatenate(parts, 0), T["pick"][...]).reshape(4, 16, 256)
     light_out[...] = jnp.where(lane == which, picked, 0.0).sum(1)
     arrived(r5, 6)
-    for c, (re, im) in enumerate(stage_e(r5[...].reshape(4, 32, 8, 128), T)):
+    for c, (re, im) in enumerate(stage_e(r5[...].astype(f32).reshape(4, 32, 8, 128), T)):
         s6[c, 0] = re.astype(bf16)
         s6[c, 1] = im.astype(bf16)
     send_cols(s6, r6, 7)
     arrived(r6, 7)
+    for slot, src in enumerate((x1, ts, s2, s3, s4, ls, s5, s6)):
+        sent(src, slot)
+
+
+def finish(r6, picked, grad, light):
     for c in range(8):
         grad[:, 32 * c:32 * c + 32, :] = r6[c].astype(f32)
-    for slot, src in enumerate((x1, ts, s2, s3, s4, ls, s5, s6)):
-        sent(src, slot)
+    for i in range(2):
+        light[i] = picked[2 * i:2 * i + 2]
 
 
 def local(slm_field, target_light):
@@ -388,20 +399,25 @@
     consts = [jnp.asarray(T[k]) for k in NAMES]
     vmem, anywhere = pl.BlockSpec(memory_space=pltpu.VMEM), pl.BlockSpec(memory_space=pl.ANY)
     V = pltpu.VMEM
-    wide, f_all, b_all = V((8, 2, 32, 256), bf16), V((128, 8, 128), f32), V((128, 16, 128), bf16)
+    wide, f_all, b_all = V((8, 2, 32, 256), bf16), V((128, 8, 128), bf16), V((128, 16, 128), bf16)
     small = V((8, 32, 128), f32)
-    gradient, light = pl.pallas_call(
+    blocks, picked = pl.pallas_call(
         body,
-        out_shape=(jax.ShapeDtypeStruct((2, 256, 256), f32), jax.ShapeDtypeStruct((4, 256), f32)),
+        out_shape=(jax.ShapeDtypeStruct((8, 2, 32, 256), bf16), jax.ShapeDtypeStruct((4, 256), f32)),
         in_specs=[vmem, vmem] + [anywhere] * len(NAMES),
-        out_specs=(vmem, vmem),
+        out_specs=(anywhere, vmem),
         scratch_shapes=[V(T[k].shape, T[k].dtype) for k in NAMES]
-        + [wide, wide, small, small, f_all, f_all, b_all, b_all, small, small, b_all, b_all, f_all, f_all, wide, wide]
+        + [wide, wide, small, small, f_all, f_all, b_all, b_all, small, small, b_all, b_all, f_all, f_all, wide]
         + [V((512, 128), f32)] * 2
         + [pltpu.SemaphoreType.DMA((len(NAMES),)), pltpu.SemaphoreType.DMA((8,)), pltpu.SemaphoreType.DMA((8,))],
         compiler_params=pltpu.CompilerParams(collective_id=0, has_side_effects=True, vmem_limit_bytes=56 << 20),
-    )(slm_field, target_light.reshape(4, 256), *consts)
-    return gradient, light.reshape(2, 2, 256)
+    )(slm_field, target_light, *consts)
+    return pl.pallas_call(
+        finish,
+        out_shape=(jax.ShapeDtypeStruct((2, 256, 256), f32), jax.ShapeDtypeStruct((2, 2, 256), f32)),
+        in_specs=[vmem, vmem],
+        out_specs=(vmem, vmem),
+    )(blocks, picked)
 
 
 def solution(mesh):

time: 76.5 us -> 68 us (0.89)
  local copies, waits for them, and re-layouts: 4.44 us -> 0 us
  Pallas kernels: 71.2 us -> 67.2 us
    pallas_call x1 -> x2, Pallas kernels: 71.2 us -> 67.2 us  [the longest x1 65.4 us: local(): pl.pallas_call(body, out_shape=(jax.ShapeDtypeStruct((8, 2, 32, 256), bf1...]
    reshape x2 -> x0, local copies, waits for them, and re-layouts: 2.57 us -> none  [the longest x1 1.29 us: local(): target_light.reshape(4, 256)]
    unnamed x1 -> x0, local copies, waits for them, and re-layouts: 1.87 us -> none
where the time goes in v1:
time: 68 us; the launch traced here: 67.8 us
  Pallas kernels  67.2 us (99%)
    pallas_call x1, Pallas kernels, local(): pl.pallas_call(body, out_shape=(jax.ShapeDtypeStruct((8, 2, 32, 256), bf1...  65.4 us
    pallas_call x1, Pallas kernels, local(): pl.pallas_call(finish, out_shape=(jax.ShapeDtypeStruct((2, 256, 256), f32...  1.78 us

profile of v1, /device:TPU:1, one launch (start us, length us, event | category | flops | bytes accessed | tf_op | source)
XLA Modules:
  0.0 67.8 jit_solution(17458252614425760592)
XLA Ops:
  0.6 65.4 %shard_map.158 = (bf16[8,2,32,256]{3,2,1,0:T(8,128)(2,1)}, f32[4,256]{1,0:T(4,128)}) custom-call(f32[2,256,256]{2,1,0:T(8,128)} %field.1, f32[2,2,256]{2,1,0:T(2,128)} %target.1, bf16[256,512]{1,0:T(8,128)(2,1)} %constant.26.clone.refs_0_, bf16[256,256]{1,0:T(8,128)(2,1)} %constant.27.clone.refs_1_, bf16[256,256]{1,0:T(8,128)(2,1)} %constant.28.clone.refs_2_, ...), custom_call_target="tpu_custom_call" | custom-call | tf_op jit(solution)/shard_map/pallas_call | solution.py:404
  66.0 1.8 %shard_map.159 = (f32[2,256,256]{2,1,0:T(8,128)}, f32[2,2,256]{2,1,0:T(2,128)}) custom-call(bf16[8,2,32,256]{3,2,1,0:T(8,128)(2,1)} %get-tuple-element.4.r6, f32[4,256]{1,0:T(4,128)} %get-tuple-element.5.picked), custom_call_target="tpu_custom_call" | custom-call | tf_op jit(solution)/shard_map/pallas_call | solution.py:415

commit v2 on v1

v2 whole, which is shorter than its diff:
```python
import math

import jax
import jax.numpy as jnp
import numpy as np
from jax import lax
from jax.experimental import pallas as pl
from jax.experimental.pallas import tpu as pltpu
from jax.sharding import PartitionSpec as P

MESH = pl.DeviceIdType.MESH

f32, bf16 = jnp.float32, jnp.bfloat16

def mm(a, b, dims=((1,), (0,))):
    return lax.dot_general(a, b, (dims, ((), ())), preferred_element_type=f32)

def roll(x, shift):
    return pltpu.roll(x, shift, x.ndim - 1)

def turn(pair, angle):
    re, im = pair
    c, s = math.cos(angle), math.sin(angle)
    if abs(s) < 1e-9:
        return (re, im) if c > 0 else (-re, -im)
    if abs(c) < 1e-9:
        return (-im, re) if s > 0 else (im, -re)
    if abs(abs(c) - abs(s)) < 1e-9:
        k = abs(c)
        a, b = (re, im) if c > 0 else (-re, -im)
        if (s > 0) == (c > 0):
            return k * (a - b), k * (a + b)
        return k * (a + b), k * (b - a)
    return re * c - im * s, re * s + im * c

def fft_list(xs, sign):
    n = len(xs)
    if n == 1:
        return list(xs)
    even, odd = fft_list(xs[0::2], sign), fft_list(xs[1::2], sign)
    out = [None] * n
    for k in range(n // 2):
        t = turn(odd[k], sign * 2 * math.pi * k / n)
        e = even[k]
        out[k] = (e[0] + t[0], e[1] + t[1])
        out[k + n // 2] = (e[0] - t[0], e[1] - t[1])
    return out

def real_fft8(x):
    s = math.sqrt(0.5)
    a0, a1 = x[0] + x[4], x[0] - x[4]
    b0, b1 = x[2] + x[6], x[2] - x[6]
    c0, c1 = x[1] + x[5], x[1] - x[5]
    d0, d1 = x[3] + x[7], x[3] - x[7]
    e1, f1 = s * (c1 - d1), s * (c1 + d1)
    r1, r3 = a1 + e1, a1 - e1
    i1, i3 = -(b1 + f1), b1 - f1
    r2, i2 = a0 - b0, d0 - c0
    p, q = a0 + b0, c0 + d0
    return [(p + q, None), (r1, i1), (r2, i2), (r3, i3), (p - q, None), (r3, -i3), (r2, -i2), (r1, -i1)]

def lane_swap(xs):
    lane = lax.broadcasted_iota(jnp.int32, xs[0].shape, xs[0].ndim - 1)
    for step, (pairs, width) in enumerate((( ((0, 1), (2, 3)), 32), (((0, 2), (1, 3)), 64))):
        low = (lane // width) % 2 == 0
        out = [None] * 4
        for lo, hi in pairs:
            out[lo] = jnp.where(low, xs[lo], roll(xs[hi], width))
            out[hi] = jnp.where(low, roll(xs[lo], 128 - width), xs[hi])
        xs = out
    return xs

def by_i(x):
    lane = lax.broadcasted_iota(jnp.int32, x.shape, x.ndim - 1)
    return jnp.where(lane < 64, -1.0, 1.0) * roll(x, 64)

def tables():
    a = np.arange(256)
    t256 = 2 * np.pi * ((a[:, None] * a[None]) % 256) / 256
    C, S = np.cos(t256), np.sin(t256)
    cs = np.concatenate([C, S], 1)
    b = np.arange(128)
    t128 = 2 * np.pi * ((b[:, None] * b[None]) % 128) / 128
    c1, s1 = np.cos(t128), np.sin(t128)
    dfwd = np.block([[c1, -s1], [s1, c1]])
    dinv = np.block([[c1, s1], [-s1, c1]])
    taper = np.sin(np.pi * (a + 0.5) / 256) ** 2
    tr = taper[:, None] * C
    ti = -taper[:, None] * S
    rr, rim = tr / 256, ti / 256
    row = np.zeros((2, 256, 4, 2, 64))
    for g in range(4):
        s = slice(64 * g, 64 * g + 64)
        row[0, :, g, 0], row[0, :, g, 1] = rr[:, s], rim[:, s]
        row[1, :, g, 0], row[1, :, g, 1] = -rim[:, s], rr[:, s]
    row = row.reshape(512, 512)
    ct = np.concatenate([tr.T, ti.T], 1)
    cth = np.concatenate([tr, ti], 1)
    v0 = np.arange(8)
    th = 2 * np.pi * v0[:, None] * a[None] / 2048
    u0 = np.arange(32)
    t4 = 2 * np.pi * u0[:, None] * b[None] / 4096
    l = np.arange(128)
    ones = ((l[:, None] % 64) // 16 == (l[None] % 64) // 16) / 256.0
    B = lambda x: x.astype(jnp.bfloat16)
    F = lambda x: x.astype(np.float32)
    return dict(cs=B(cs), dfwd=B(dfwd), dinv=B(dinv), row=B(row), rowh=B(row.T.copy()), ct=B(ct), cth=B(cth),
                tw=F(np.stack([np.cos(th), np.sin(th)])),
                twl=F(np.broadcast_to(np.stack([np.cos(th), np.sin(th)])[..., None], (2, 8, 256, 128))),
                t4=F(np.stack([np.cos(t4), np.sin(t4)])), ones=B(ones))

def filt(me):
    q, k = me // 32, me % 32
    u0 = lax.broadcasted_iota(jnp.int32, (32, 16, 128), 0)
    w = lax.broadcasted_iota(jnp.int32, (32, 16, 128), 1)
    u1 = lax.broadcasted_iota(jnp.int32, (32, 16, 128), 2)
    u = 32 * u1 + u0
    v = 8 * (8 * k + w % 8) + 2 * q + w // 8
    fx = jnp.where(u < 2048, u, u - 4096).astype(f32) / 4096
    fy = jnp.where(v < 1024, v, v - 2048).astype(f32) / 2048
    s = fx * fx + fy * fy
    turns = 16000.0 * s / (jnp.sqrt(225.0 - s) + 15.0)
    quarters = 4.0 * (turns - jnp.floor(turns))
    nearest = jnp.floor(quarters + 0.5)
    z = (quarters - nearest) * (math.pi / 2)
    n = nearest.astype(jnp.int32)
    zz = z * z
    sine = z * (1 + zz * (-1 / 6 + zz * (1 / 120 + zz * (-1 / 5040 + zz / 362880))))
    cosine = 1 + zz * (-1 / 2 + zz * (1 / 24 + zz * (-1 / 720 + zz / 40320)))
    odd = n % 2 == 1
    c, d = jnp.where(odd, sine, cosine), jnp.where(odd, cosine, sine)
    half = 2.0 ** -23
    c = jnp.where((n % 4 == 1) | (n % 4 == 2), -half, half) * c
    d = jnp.where(n % 4 >= 2, half, -half) * d
    return c.reshape(512, 128), d.reshape(512, 128)

def turn_row(table, v):
    return table[0, v], table[1, v]


def columns(xs, T, kr, ki, sign):
    z = fft_list(xs, -1)
    lhs = []
    for u in range(32):
        c, s = T["t4"][0, u:u + 1], T["t4"][1, u:u + 1]
        re, im = z[u]
        lhs.append(jnp.concatenate([re * c + im * s, im * c - re * s], 1).astype(bf16))
    f = mm(jnp.concatenate(lhs, 0), T["dfwd"][...])
    fr, fi = f[:, :128], f[:, 128:]
    if sign > 0:
        pr, pi = fr * kr - fi * ki, fr * ki + fi * kr
    else:
        pr, pi = fr * kr + fi * ki, fi * kr - fr * ki
    g = mm(jnp.concatenate([pr, pi], 1).astype(bf16), T["dinv"][...])
    ys = []
    for u in range(32):
        c, s = T["t4"][0, u:u + 1], T["t4"][1, u:u + 1]
        re, im = g[16 * u:16 * u + 16, :128], g[16 * u:16 * u + 16, 128:]
        ys.append((re * c - im * s, im * c + re * s))
    return fft_list(ys, 1)


def halves(x, table):
    hi = x.astype(bf16)
    return mm(hi, table) + mm((x - hi.astype(f32)).astype(bf16), table)


NAMES = ("tw", "cs", "spread", "t4", "dfwd", "dinv", "row", "twl", "ct", "ones", "cth", "pick", "rowh")


def body(field, target, *refs):
    n = len(NAMES)
    hbm, refs = dict(zip(NAMES, refs[:n])), refs[n:]
    r6, light_out = refs[:2]
    T, refs = dict(zip(NAMES, refs[2:2 + n])), refs[2 + n:]
    (x0, tv, x1, r1, tr, goals, ra, s2, r2, xr, xi, nr, ni, s3, r3, ps, qs, nb, jb, sp, bk, hs, ls, lr, s4, r4, od, s5, r5,
     zr, zi, s6, kr, ki, tsem, ssem, rsem) = refs
    row, col = lax.axis_index("rows"), lax.axis_index("cols")
    z, high, low = 2 * (row & 1) + (col >> 2), row >> 1, col & 3
    me = 32 * z + 4 * high + low
    highs, lows = [(high + a) & 7 for a in range(8)], [(low + b) & 3 for b in range(4)]
    barrier = pltpu.get_barrier_semaphore()
    for k in range(1, 16):
        pl.semaphore_signal(barrier, inc=1, device_id=((row + k) & 15, col), device_id_type=MESH)
    for k in range(1, 8):
        pl.semaphore_signal(barrier, inc=1, device_id=(row, (col + k) & 7), device_id_type=MESH)
    first = [pltpu.make_async_copy(field, x0, tsem.at[n]), pltpu.make_async_copy(target, tv, tsem.at[n + 1])]
    loads = [pltpu.make_async_copy(hbm[k], T[k], tsem.at[i]) for i, k in enumerate(NAMES)]
    for copy in first + loads:
        copy.start()

    def need(*names):
        for k in names:
            loads[NAMES.index(k)].wait()

    def copy_to(src, dst, send, recv, d):
        return pltpu.make_async_remote_copy(src, dst, ssem.at[send], rsem.at[recv], device_id=d, device_id_type=MESH)

    def send_cols(src, dst, send, recv):
        for k in range(1, 8):
            d = (col + k) & 7
            copy_to(src(d), dst.at[col], send, recv, (row, d)).start()

    def send_group(src, dst, send, recv, j):
        q = ahead(j)
        up, left = q >> 1, 4 * (q & 1)
        for b in range(4):
            for a in range(8):
                if a or b or j:
                    d = 32 * q + 4 * highs[a] + lows[b]
                    copy_to(src(d, q, a, b), dst.at[me], send, recv + j, (2 * highs[a] + up, left + lows[b])).start()

    def arrived(dst, count, slot):
        some = dst.at[pl.ds(0, count)]
        copy_to(some, some, 0, slot, (row, col)).wait_recv()

    def sent(src, count, slot):
        some = src.at[pl.ds(0, count)]
        copy_to(some, some, slot, 0, (row, col)).wait_send()

    def ahead(j):
        return (z + j) & 3

    def behind(j):
        return (z + 4 - j) & 3

    for copy in first:
        copy.wait()
    for c in range(8):
        x1[c] = x0[:, 32 * c:32 * c + 32, :].astype(bf16)
    pl.semaphore_wait(barrier, 22)
    send_cols(lambda d: x1.at[d], r1, 0, 0)
    send_cols(lambda d: tv, tr, 1, 1)
    r1[pl.ds(col, 1)] = x1[pl.ds(col, 1)]
    tr[pl.ds(col, 1)] = tv[...][None]
    a, b = filt(me)
    kr[...] = a
    ki[...] = b

    need("tw", "cs")
    arrived(r1, 7, 0)
    zs = fft_list([(r1[c, 0].astype(f32), r1[c, 1].astype(f32)) for c in range(8)], -1)
    for v in range(8):
        q, w = v // 2, 32 * (v % 2)
        c, s = turn_row(T["tw"], v)
        re, im = zs[v]
        if v:
            re, im = re * c + im * s, im * c - re * s
        ra[q, w:w + 32] = jnp.concatenate([re, im], 1).astype(bf16)
        ra[q, 64 + w:96 + w] = jnp.concatenate([im, -re], 1).astype(bf16)
    for j in range(4):
        q = ahead(j)
        y = mm(T["cs"][...], ra[q], ((1,), (1,)))
        s2[pl.ds(32 * q, 32)] = y.reshape(32, 8, 128).astype(bf16)
        send_group(lambda d, *_: s2.at[d], r2, 2, 2, j)
        if j == 0:
            r2[pl.ds(me, 1)] = s2[pl.ds(me, 1)]

    need("spread")
    arrived(tr, 7, 1)
    lane = lax.broadcasted_iota(jnp.int32, (256, 256), 1) % 16
    which = lax.broadcasted_iota(jnp.int32, (256, 256), 0) % 16
    group = col & 3
    mine = [tr[c, pl.ds(col >> 2, 1)] for c in range(8)]
    rows = [jnp.broadcast_to(mine[j // 2][0, j % 2:j % 2 + 1], (16, 256)) for j in range(16)]
    goals[...] = halves(jnp.where(lane == which, jnp.concatenate(rows, 0), 0.0), T["spread"][group])

    need("t4", "dfwd", "dinv")
    for j in range(4):
        q = behind(j)
        arrived(r2, 32 if j else 31, 2 + j)
        x = r2[pl.ds(32 * q, 32)].astype(f32).reshape(8, 4, 8, 128)
        b = lane_swap([x[:, g] for g in range(4)])
        for v in range(2):
            xr[q, :, 8 * v:8 * v + 8] = b[v]
            xi[q, :, 8 * v:8 * v + 8] = b[2 + v]
    xs = [(xr[i % 4, i // 4], xi[i % 4, i // 4]) for i in range(32)]
    for i, (re, im) in enumerate(columns(xs, T, kr[...], ki[...], 1)):
        k = (i - 1) % 32
        for x, part in ((nr, re.astype(bf16)), (ni, im.astype(bf16))):
            x[0, i % 4, i // 4] = part
            x[1, k % 4, k // 4] = part
    need("row")
    for j in range(4):
        q = ahead(j)
        parts = [x[d, q].reshape(128, 128) for x in (nr, ni) for d in range(2)]
        o = mm(jnp.concatenate(parts, 1), T["row"][...])
        for g in range(4):
            s3[pl.ds(8 * q, 8), g] = o[:, 128 * g:128 * g + 128].reshape(8, 16, 128).astype(bf16)
        send_group(lambda d, q, a, b: s3.at[8 * q + highs[a], lows[b]], r3, 3, 6, j)
        if j == 0:
            r3[pl.ds(me, 1)] = s3[8 * z + high, pl.ds(low, 1)]

    need("twl", "ct", "ones", "cth", "pick", "rowh")
    for j in range(4):
        q = behind(j)
        arrived(r3, 32 if j else 31, 6 + j)
        x = r3[pl.ds(32 * q, 32)].astype(f32).reshape(32, 2, 8, 128)
        cols = []
        for v in range(2):
            xv = x[:, v].reshape(256, 128)
            cols.append(jnp.concatenate([xv.astype(bf16), by_i(xv).astype(bf16)], 0))
        o = mm(T["cs"][...], jnp.concatenate(cols, 1))
        for v in range(2):
            zv = o[:, 128 * v:128 * v + 128]
            ps[2 * q + v] = zv * T["twl"][0, 2 * q + v]
            qs[2 * q + v] = zv * T["twl"][1, 2 * q + v]
    for m in range(0, 256, 32):
        part = slice(m, m + 32)
        for c, (p, q) in enumerate(fft_list([(ps[v, part], qs[v, part]) for v in range(8)], 1)):
            near = p + by_i(q)
            nb[c, part] = near.astype(bf16)
            jb[c, part] = by_i(near).astype(bf16)
    sums = []
    for c in range(8):
        d = (c + 1) % 8
        even = jnp.concatenate([nb[c], jb[c]], 0)
        odd = jnp.concatenate([nb[c, 128:], nb[d, :128], jb[c, 128:], jb[d, :128]], 0)
        o = mm(T["ct"][...], jnp.concatenate([even, odd], 1))
        for j in range(2):
            s = o[:, 128 * j:128 * j + 128]
            sp[2 * c + j] = s
            sums.append((s * s).reshape(16, 16, 128).sum(1))
    light = halves(jnp.concatenate(sums, 0), T["ones"][...])
    wt = 4.0 * (light - goals[...])
    for c in range(8):
        cols = []
        for j in (2 * c, 2 * c + 1):
            w = sp[j] * jnp.concatenate([jnp.broadcast_to(wt[r:r + 1], (16, 128)) for r in range(16 * j, 16 * j + 16)], 0)
            cols.append(jnp.concatenate([w.astype(bf16), (-by_i(w)).astype(bf16)], 0))
        o = mm(T["cth"][...], jnp.concatenate(cols, 1))
        bk[2 * c] = o[:, :128]
        bk[2 * c + 1] = o[:, 128:]
    for m in range(0, 256, 32):
        part = slice(m, m + 32)
        xs = []
        for c in range(8):
            if m < 128:
                xs.append(bk[2 * c, part] + bk[(2 * c - 1) % 16, m + 128:m + 160])
            else:
                xs.append(bk[2 * c + 1, m - 128:m - 96] + bk[2 * c, part])
        for v, (e, f) in enumerate(real_fft8(xs)):
            c, s = T["twl"][0, v, part], T["twl"][1, v, part]
            if f is None:
                p, q = e * c, -e * s
            else:
                p, q = e * c + f * s, f * c - e * s
            h = p + by_i(q)
            w = slice(128 * (v % 2), 128 * (v % 2) + 128)
            hs[v // 2, part, w] = h.astype(bf16)
            hs[v // 2, 256 + m:288 + m, w] = (-by_i(h)).astype(bf16)
    for j in range(4):
        q = ahead(j)
        y = mm(T["cs"][...], hs[q])
        pair = [y[:, 128 * v:128 * v + 128].reshape(32, 1, 8, 128) for v in range(2)]
        s4[pl.ds(32 * q, 32)] = jnp.concatenate(pair, 1).reshape(32, 16, 128).astype(bf16)
        send_group(lambda d, *_: s4.at[d], r4, 4, 10, j)
        if j == 0:
            r4[pl.ds(me, 1)] = s4[pl.ds(me, 1)]
    views = jnp.where(lane == which, halves(light, T["pick"][group]), 0.0).reshape(16, 16, 256).sum(1)
    for c in range(8):
        ls[c] = views[2 * c:2 * c + 2]
    send_cols(lambda d: ls.at[d], lr, 5, 14)
    lr[pl.ds(col, 1)] = ls[pl.ds(col, 1)]

    for j in range(4):
        q = behind(j)
        arrived(r4, 32 if j else 31, 10 + j)
        x = r4[pl.ds(32 * q, 32)].reshape(8, 4, 16, 128)
        o = mm(jnp.concatenate([x[:, g].reshape(128, 128) for g in range(4)], 1), T["rowh"][...])
        od[q] = o.reshape(8, 16, 512)
    xs = []
    for i in range(32):
        a, b, k = i % 4, i // 4, (i - 1) % 32
        c, d = k % 4, k // 4
        xs.append((od[a, b, :, :128] + od[c, d, :, 128:256], od[a, b, :, 256:384] + od[c, d, :, 384:]))
    for i, (re, im) in enumerate(columns(xs, T, kr[...], ki[...], -1)):
        xr[i % 4, i // 4] = re
        xi[i % 4, i // 4] = im
    for j in range(4):
        q = ahead(j)
        parts = lane_swap([x[q, :, 8 * v:8 * v + 8] for x in (xr, xi) for v in range(2)])
        for g in range(4):
            s5[pl.ds(8 * q, 8), g] = parts[g].astype(bf16)
        send_group(lambda d, q, a, b: s5.at[8 * q + highs[a], lows[b]], r5, 6, 15, j)
        if j == 0:
            r5[pl.ds(me, 1)] = s5[8 * z + high, pl.ds(low, 1)]
    arrived(lr, 7, 14)
    for i in range(2):
        light_out[2 * i:2 * i + 2] = (lr[4 * i] + lr[4 * i + 1]) + (lr[4 * i + 2] + lr[4 * i + 3])

    for j in range(4):
        q = behind(j)
        arrived(r5, 32 if j else 31, 15 + j)
        x = r5[pl.ds(32 * q, 32)].astype(f32).reshape(256, 128).T.astype(bf16)
        o = mm(x, T["cs"][...])
        for v in range(2):
            pr, pi = o[32 * v:32 * v + 32], o[64 + 32 * v:96 + 32 * v]
            re, im = pr[:, :256] - pi[:, 256:], pi[:, :256] + pr[:, 256:]
            c, s = turn_row(T["tw"], 2 * q + v)
            zr[2 * q + v] = re * c - im * s
            zi[2 * q + v] = im * c + re * s
    for c, (re, im) in enumerate(fft_list([(zr[v], zi[v]) for v in range(8)], 1)):
        s6[c, 0] = re.astype(bf16)
        s6[c, 1] = im.astype(bf16)
    send_cols(lambda d: s6.at[d], r6, 7, 19)
    own = pltpu.make_async_copy(s6.at[col], r6.at[col], tsem.at[0])
    own.start()
    for slot, (src, count) in enumerate(((x1, 7), (tr, 7), (r2, 127), (r3, 127), (r4, 127), (ls, 7), (r5, 127), (s6, 7))):
        sent(src, count, slot)
    own.wait()
    arrived(r6, 7, 19)


def finish(blocks, picked, grad, light):
    for c in range(8):
        grad[:, 32 * c:32 * c + 32, :] = blocks[c].astype(f32)
    for i in range(2):
        light[i] = picked[2 * i:2 * i + 2]


def local(slm_field, target_light):
    T = tables()
    T["tw"] = T["tw"].reshape(2, 8, 1, 256)
    view, lane = np.arange(256) // 16, np.arange(128)
    spread = np.stack([view[:, None] == 4 * g + (lane % 64) // 16 for g in range(4)])
    T["spread"] = spread.astype(jnp.bfloat16)
    T["pick"] = (spread & (lane % 16 == 0) & (lane < 64)).transpose(0, 2, 1).astype(jnp.bfloat16)
    consts = [jnp.asarray(T[k]) for k in NAMES]
    vmem, anywhere = pl.BlockSpec(memory_space=pltpu.VMEM), pl.BlockSpec(memory_space=pl.ANY)
    V = pltpu.VMEM
    block, f_all, b_all = V((8, 2, 32, 256), bf16), V((128, 8, 128), bf16), V((128, 16, 128), bf16)
    line, lines = V((8, 256, 128), bf16), V((8, 256, 128), f32)
    scratch = dict(
        x0=V((2, 256, 256), f32), tv=V((2, 2, 256), f32), x1=block, r1=block, tr=V((8, 2, 2, 256), f32), goals=V((256, 128), f32),
        ra=V((4, 128, 512), bf16), s2=f_all, r2=f_all, xr=V((4, 8, 16, 128), f32), xi=V((4, 8, 16, 128), f32),
        nr=V((2, 4, 8, 16, 128), bf16), ni=V((2, 4, 8, 16, 128), bf16), s3=V((32, 4, 16, 128), bf16), r3=b_all, ps=lines, qs=lines,
        nb=line, jb=line, sp=V((16, 256, 128), f32), bk=V((16, 256, 128), f32), hs=V((4, 512, 256), bf16),
        ls=V((8, 2, 256), f32), lr=V((8, 2, 256), f32), s4=b_all, r4=b_all, od=V((4, 8, 16, 512), f32),
        s5=V((32, 4, 8, 128), bf16), r5=f_all, zr=V((8, 32, 256), f32), zi=V((8, 32, 256), f32), s6=block,
        kr=V((512, 128), f32), ki=V((512, 128), f32),
    )
    blocks, picked = pl.pallas_call(
        body,
        out_shape=(jax.ShapeDtypeStruct((8, 2, 32, 256), bf16), jax.ShapeDtypeStruct((4, 256), f32)),
        in_specs=[anywhere] * (2 + len(NAMES)),
        out_specs=(anywhere, vmem),
        scratch_shapes=[V(T[k].shape, T[k].dtype) for k in NAMES]
        + list(scratch.values())
        + [pltpu.SemaphoreType.DMA((len(NAMES) + 2,)), pltpu.SemaphoreType.DMA((8,)), pltpu.SemaphoreType.DMA((20,))],
        compiler_params=pltpu.CompilerParams(collective_id=0, has_side_effects=True, vmem_limit_bytes=60 << 20),
    )(slm_field, target_light, *consts)
    return pl.pallas_call(
        finish,
        out_shape=(jax.ShapeDtypeStruct((2, 256, 256), f32), jax.ShapeDtypeStruct((2, 2, 256), f32)),
        in_specs=[vmem, vmem],
        out_specs=(vmem, vmem),
    )(blocks, picked)


def solution(mesh):
    return jax.shard_map(
        local,
        mesh=mesh,
        in_specs=(P(None, "rows", "cols"), P("rows", "cols", None)),
        out_specs=(P(None, "rows", "cols"), P("rows", "cols", None)),
        check_vma=False,
    )
```

time: 68 us -> 65.1 us (0.957)
  Pallas kernels: 67.2 us -> 64.3 us
    pallas_call x1, Pallas kernels: 65.4 us -> 62.5 us  [local(): pl.pallas_call(body, out_shape=(jax.ShapeDtypeStruct((8, 2, 32, 256), bf1...]
where the time goes in v2:
time: 65.1 us; the launch traced here: 64.9 us
  Pallas kernels  64.3 us (99%)
    pallas_call x1, Pallas kernels, local(): pl.pallas_call(body, out_shape=(jax.ShapeDtypeStruct((8, 2, 32, 256), bf1...  62.5 us
    pallas_call x1, Pallas kernels, local(): pl.pallas_call(finish, out_shape=(jax.ShapeDtypeStruct((2, 256, 256), f32...  1.78 us

profile of v2, /device:TPU:1, one launch (start us, length us, event | category | flops | bytes accessed | tf_op | source)
XLA Modules:
  0.0 64.9 jit_solution(212677236285723800)
XLA Ops:
  0.6 62.5 %shard_map.158 = (bf16[8,2,32,256]{3,2,1,0:T(8,128)(2,1)}, f32[4,256]{1,0:T(4,128)}) custom-call(f32[2,256,256]{2,1,0:T(8,128)} %field.1, f32[2,2,256]{2,1,0:T(2,128)} %target.1, f32[2,8,1,256]{3,2,1,0:T(1,128)} %constant.26.clone.refs_0_, bf16[256,512]{1,0:T(8,128)(2,1)} %constant.27.clone.refs_1_, bf16[4,256,128]{2,1,0:T(8,128)(2,1)} %constant.28.clone.refs_2_, ...), custom_call_target="tpu_custom_call" | custom-call | tf_op jit(solution)/shard_map/pallas_call | solution.py:443
  63.1 1.8 %shard_map.159 = (f32[2,256,256]{2,1,0:T(8,128)}, f32[2,2,256]{2,1,0:T(2,128)}) custom-call(bf16[8,2,32,256]{3,2,1,0:T(8,128)(2,1)} %get-tuple-element.4.blocks, f32[4,256]{1,0:T(4,128)} %get-tuple-element.5.picked), custom_call_target="tpu_custom_call" | custom-call | tf_op jit(solution)/shard_map/pallas_call | solution.py:453

commit v3 on v2

--- a/solution.py
+++ b/solution.py
@@ -134,6 +134,14 @@
     d = jnp.where(n % 4 >= 2, half, -half) * d
     return c.reshape(512, 128), d.reshape(512, 128)
 
+FAR_FIRST = sorted(
+    ((a, b) for a in range(8) for b in range(4)),
+    key=lambda p: -(min(p[0] >> 1, 4 - (p[0] >> 1)) + 2 * (p[0] & 1) + min(p[1], 4 - p[1])),
+)
+QUARTERS = (2, 3, 1, 0)
+STEP = 8
+
+
 def turn_row(table, v):
     return table[0, v], table[1, v]
 
@@ -178,7 +186,8 @@
     row, col = lax.axis_index("rows"), lax.axis_index("cols")
     z, high, low = 2 * (row & 1) + (col >> 2), row >> 1, col & 3
     me = 32 * z + 4 * high + low
-    highs, lows = [(high + a) & 7 for a in range(8)], [(low + b) & 3 for b in range(4)]
+    highs = [((high + (a & 6)) & 6) + ((high + a) & 1) for a in range(8)]
+    lows = [(low + b) & 3 for b in range(4)]
     barrier = pltpu.get_barrier_semaphore()
     for k in range(1, 16):
         pl.semaphore_signal(barrier, inc=1, device_id=((row + k) & 15, col), device_id_type=MESH)
@@ -197,18 +206,17 @@
         return pltpu.make_async_remote_copy(src, dst, ssem.at[send], rsem.at[recv], device_id=d, device_id_type=MESH)
 
     def send_cols(src, dst, send, recv):
-        for k in range(1, 8):
-            d = (col + k) & 7
+        for k in (4, 1, 5, 3, 6, 2, 7):
+            d = ((col ^ k) & 4) + ((col + k) & 3)
             copy_to(src(d), dst.at[col], send, recv, (row, d)).start()
 
     def send_group(src, dst, send, recv, j):
         q = ahead(j)
         up, left = q >> 1, 4 * (q & 1)
-        for b in range(4):
-            for a in range(8):
-                if a or b or j:
-                    d = 32 * q + 4 * highs[a] + lows[b]
-                    copy_to(src(d, q, a, b), dst.at[me], send, recv + j, (2 * highs[a] + up, left + lows[b])).start()
+        for a, b in FAR_FIRST:
+            if a or b or QUARTERS[j]:
+                d = 32 * q + 4 * highs[a] + lows[b]
+                copy_to(src(d, q, a, b), dst.at[me], send, recv + j, (2 * highs[a] + up, left + lows[b])).start()
 
     def arrived(dst, count, slot):
         some = dst.at[pl.ds(0, count)]
@@ -219,10 +227,10 @@
         copy_to(some, some, slot, 0, (row, col)).wait_send()
 
     def ahead(j):
-        return (z + j) & 3
+        return z ^ QUARTERS[j]
 
     def behind(j):
-        return (z + 4 - j) & 3
+        return z ^ QUARTERS[j]
 
     for copy in first:
         copy.wait()
@@ -253,7 +261,7 @@
         y = mm(T["cs"][...], ra[q], ((1,), (1,)))
         s2[pl.ds(32 * q, 32)] = y.reshape(32, 8, 128).astype(bf16)
         send_group(lambda d, *_: s2.at[d], r2, 2, 2, j)
-        if j == 0:
+        if QUARTERS[j] == 0:
             r2[pl.ds(me, 1)] = s2[pl.ds(me, 1)]
 
     need("spread")
@@ -268,7 +276,7 @@
     need("t4", "dfwd", "dinv")
     for j in range(4):
         q = behind(j)
-        arrived(r2, 32 if j else 31, 2 + j)
+        arrived(r2, 32 if QUARTERS[j] else 31, 2 + j)
         x = r2[pl.ds(32 * q, 32)].astype(f32).reshape(8, 4, 8, 128)
         b = lane_swap([x[:, g] for g in range(4)])
         for v in range(2):
@@ -288,13 +296,13 @@
         for g in range(4):
             s3[pl.ds(8 * q, 8), g] = o[:, 128 * g:128 * g + 128].reshape(8, 16, 128).astype(bf16)
         send_group(lambda d, q, a, b: s3.at[8 * q + highs[a], lows[b]], r3, 3, 6, j)
-        if j == 0:
+        if QUARTERS[j] == 0:
             r3[pl.ds(me, 1)] = s3[8 * z + high, pl.ds(low, 1)]
 
     need("twl", "ct", "ones", "cth", "pick", "rowh")
     for j in range(4):
         q = behind(j)
-        arrived(r3, 32 if j else 31, 6 + j)
+        arrived(r3, 32 if QUARTERS[j] else 31, 6 + j)
         x = r3[pl.ds(32 * q, 32)].astype(f32).reshape(32, 2, 8, 128)
         cols = []
         for v in range(2):
@@ -311,26 +319,31 @@
             near = p + by_i(q)
             nb[c, part] = near.astype(bf16)
             jb[c, part] = by_i(near).astype(bf16)
-    sums = []
-    for c in range(8):
-        d = (c + 1) % 8
-        even = jnp.concatenate([nb[c], jb[c]], 0)
-        odd = jnp.concatenate([nb[c, 128:], nb[d, :128], jb[c, 128:], jb[d, :128]], 0)
-        o = mm(T["ct"][...], jnp.concatenate([even, odd], 1))
-        for j in range(2):
-            s = o[:, 128 * j:128 * j + 128]
-            sp[2 * c + j] = s
-            sums.append((s * s).reshape(16, 16, 128).sum(1))
-    light = halves(jnp.concatenate(sums, 0), T["ones"][...])
-    wt = 4.0 * (light - goals[...])
-    for c in range(8):
-        cols = []
-        for j in (2 * c, 2 * c + 1):
-            w = sp[j] * jnp.concatenate([jnp.broadcast_to(wt[r:r + 1], (16, 128)) for r in range(16 * j, 16 * j + 16)], 0)
-            cols.append(jnp.concatenate([w.astype(bf16), (-by_i(w)).astype(bf16)], 0))
-        o = mm(T["cth"][...], jnp.concatenate(cols, 1))
-        bk[2 * c] = o[:, :128]
-        bk[2 * c + 1] = o[:, 128:]
+    lights = []
+    for first in range(0, 8, STEP):
+        sums = []
+        for c in range(first, first + STEP):
+            d = (c + 1) % 8
+            even = jnp.concatenate([nb[c], jb[c]], 0)
+            odd = jnp.concatenate([nb[c, 128:], nb[d, :128], jb[c, 128:], jb[d, :128]], 0)
+            o = mm(T["ct"][...], jnp.concatenate([even, odd], 1))
+            for j in range(2):
+                s = o[:, 128 * j:128 * j + 128]
+                sp[2 * c + j] = s
+                sums.append((s * s).reshape(16, 16, 128).sum(1))
+        light = halves(jnp.concatenate(sums, 0), T["ones"][...])
+        wt = 4.0 * (light - goals[32 * first:32 * first + 32 * STEP])
+        lights.append(light)
+        for c in range(first, first + STEP):
+            cols = []
+            for j in (2 * c, 2 * c + 1):
+                rows = range(16 * j - 32 * first, 16 * j - 32 * first + 16)
+                w = sp[j] * jnp.concatenate([jnp.broadcast_to(wt[r:r + 1], (16, 128)) for r in rows], 0)
+                cols.append(jnp.concatenate([w.astype(bf16), (-by_i(w)).astype(bf16)], 0))
+            o = mm(T["cth"][...], jnp.concatenate(cols, 1))
+            bk[2 * c] = o[:, :128]
+            bk[2 * c + 1] = o[:, 128:]
+    light = jnp.concatenate(lights, 0)
     for m in range(0, 256, 32):
         part = slice(m, m + 32)
         xs = []
@@ -355,7 +368,7 @@
         pair = [y[:, 128 * v:128 * v + 128].reshape(32, 1, 8, 128) for v in range(2)]
         s4[pl.ds(32 * q, 32)] = jnp.concatenate(pair, 1).reshape(32, 16, 128).astype(bf16)
         send_group(lambda d, *_: s4.at[d], r4, 4, 10, j)
-        if j == 0:
+        if QUARTERS[j] == 0:
             r4[pl.ds(me, 1)] = s4[pl.ds(me, 1)]
     views = jnp.where(lane == which, halves(light, T["pick"][group]), 0.0).reshape(16, 16, 256).sum(1)
     for c in range(8):
@@ -365,7 +378,7 @@
 
     for j in range(4):
         q = behind(j)
-        arrived(r4, 32 if j else 31, 10 + j)
+        arrived(r4, 32 if QUARTERS[j] else 31, 10 + j)
         x = r4[pl.ds(32 * q, 32)].reshape(8, 4, 16, 128)
         o = mm(jnp.concatenate([x[:, g].reshape(128, 128) for g in range(4)], 1), T["rowh"][...])
         od[q] = o.reshape(8, 16, 512)
@@ -383,7 +396,7 @@
         for g in range(4):
             s5[pl.ds(8 * q, 8), g] = parts[g].astype(bf16)
         send_group(lambda d, q, a, b: s5.at[8 * q + highs[a], lows[b]], r5, 6, 15, j)
-        if j == 0:
+        if QUARTERS[j] == 0:
             r5[pl.ds(me, 1)] = s5[8 * z + high, pl.ds(low, 1)]
     arrived(lr, 7, 14)
     for i in range(2):
@@ -391,7 +404,7 @@
 
     for j in range(4):
         q = behind(j)
-        arrived(r5, 32 if j else 31, 15 + j)
+        arrived(r5, 32 if QUARTERS[j] else 31, 15 + j)
         x = r5[pl.ds(32 * q, 32)].astype(f32).reshape(256, 128).T.astype(bf16)
         o = mm(x, T["cs"][...])
         for v in range(2):

time: 65.1 us -> 61.7 us (0.948)
  Pallas kernels: 64.3 us -> 60.5 us
    pallas_call x1, Pallas kernels: 62.5 us -> 58.7 us  [local(): pl.pallas_call(body, out_shape=(jax.ShapeDtypeStruct((8, 2, 32, 256), bf1...]
where the time goes in v3:
time: 61.7 us; the launch traced here: 61.2 us
  Pallas kernels  60.5 us (98%)
  between operations  0.64 us (1%)
    pallas_call x1, Pallas kernels, local(): pl.pallas_call(body, out_shape=(jax.ShapeDtypeStruct((8, 2, 32, 256), bf1...  58.7 us
    pallas_call x1, Pallas kernels, local(): pl.pallas_call(finish, out_shape=(jax.ShapeDtypeStruct((2, 256, 256), f32...  1.78 us

profile of v3, /device:TPU:1, one launch (start us, length us, event | category | flops | bytes accessed | tf_op | source)
XLA Modules:
  0.0 61.2 jit_solution(10673643119853908726)
XLA Ops:
  0.6 58.7 %shard_map.158 = (bf16[8,2,32,256]{3,2,1,0:T(8,128)(2,1)}, f32[4,256]{1,0:T(4,128)}) custom-call(f32[2,256,256]{2,1,0:T(8,128)} %field.1, f32[2,2,256]{2,1,0:T(2,128)} %target.1, f32[2,8,1,256]{3,2,1,0:T(1,128)} %constant.26.clone.refs_0_, bf16[256,512]{1,0:T(8,128)(2,1)} %constant.27.clone.refs_1_, bf16[4,256,128]{2,1,0:T(8,128)(2,1)} %constant.28.clone.refs_2_, ...), custom_call_target="tpu_custom_call" | custom-call | tf_op jit(solution)/shard_map/pallas_call | solution.py:456
  59.4 1.8 %shard_map.159 = (f32[2,256,256]{2,1,0:T(8,128)}, f32[2,2,256]{2,1,0:T(2,128)}) custom-call(bf16[8,2,32,256]{3,2,1,0:T(8,128)(2,1)} %get-tuple-element.4.blocks, f32[4,256]{1,0:T(4,128)} %get-tuple-element.5.picked), custom_call_target="tpu_custom_call" | custom-call | tf_op jit(solution)/shard_map/pallas_call | solution.py:466

commit v4 on v3

--- a/solution.py
+++ b/solution.py
@@ -259,7 +259,7 @@
     for j in range(4):
         q = ahead(j)
         y = mm(T["cs"][...], ra[q], ((1,), (1,)))
-        s2[pl.ds(32 * q, 32)] = y.reshape(32, 8, 128).astype(bf16)
+        s2[pl.ds(32 * q, 32)] = y.reshape(32, 8, 128)
         send_group(lambda d, *_: s2.at[d], r2, 2, 2, j)
         if QUARTERS[j] == 0:
             r2[pl.ds(me, 1)] = s2[pl.ds(me, 1)]
@@ -277,7 +277,7 @@
     for j in range(4):
         q = behind(j)
         arrived(r2, 32 if QUARTERS[j] else 31, 2 + j)
-        x = r2[pl.ds(32 * q, 32)].astype(f32).reshape(8, 4, 8, 128)
+        x = r2[pl.ds(32 * q, 32)].reshape(8, 4, 8, 128)
         b = lane_swap([x[:, g] for g in range(4)])
         for v in range(2):
             xr[q, :, 8 * v:8 * v + 8] = b[v]
@@ -394,7 +394,7 @@
         q = ahead(j)
         parts = lane_swap([x[q, :, 8 * v:8 * v + 8] for x in (xr, xi) for v in range(2)])
         for g in range(4):
-            s5[pl.ds(8 * q, 8), g] = parts[g].astype(bf16)
+            s5[pl.ds(8 * q, 8), g] = parts[g]
         send_group(lambda d, q, a, b: s5.at[8 * q + highs[a], lows[b]], r5, 6, 15, j)
         if QUARTERS[j] == 0:
             r5[pl.ds(me, 1)] = s5[8 * z + high, pl.ds(low, 1)]
@@ -405,7 +405,7 @@
     for j in range(4):
         q = behind(j)
         arrived(r5, 32 if QUARTERS[j] else 31, 15 + j)
-        x = r5[pl.ds(32 * q, 32)].astype(f32).reshape(256, 128).T.astype(bf16)
+        x = r5[pl.ds(32 * q, 32)].reshape(256, 128).T.astype(bf16)
         o = mm(x, T["cs"][...])
         for v in range(2):
             pr, pi = o[32 * v:32 * v + 32], o[64 + 32 * v:96 + 32 * v]
@@ -442,7 +442,7 @@
     consts = [jnp.asarray(T[k]) for k in NAMES]
     vmem, anywhere = pl.BlockSpec(memory_space=pltpu.VMEM), pl.BlockSpec(memory_space=pl.ANY)
     V = pltpu.VMEM
-    block, f_all, b_all = V((8, 2, 32, 256), bf16), V((128, 8, 128), bf16), V((128, 16, 128), bf16)
+    block, f_all, b_all = V((8, 2, 32, 256), bf16), V((128, 8, 128), f32), V((128, 16, 128), bf16)
     line, lines = V((8, 256, 128), bf16), V((8, 256, 128), f32)
     scratch = dict(
         x0=V((2, 256, 256), f32), tv=V((2, 2, 256), f32), x1=block, r1=block, tr=V((8, 2, 2, 256), f32), goals=V((256, 128), f32),
@@ -450,7 +450,7 @@
         nr=V((2, 4, 8, 16, 128), bf16), ni=V((2, 4, 8, 16, 128), bf16), s3=V((32, 4, 16, 128), bf16), r3=b_all, ps=lines, qs=lines,
         nb=line, jb=line, sp=V((16, 256, 128), f32), bk=V((16, 256, 128), f32), hs=V((4, 512, 256), bf16),
         ls=V((8, 2, 256), f32), lr=V((8, 2, 256), f32), s4=b_all, r4=b_all, od=V((4, 8, 16, 512), f32),
-        s5=V((32, 4, 8, 128), bf16), r5=f_all, zr=V((8, 32, 256), f32), zi=V((8, 32, 256), f32), s6=block,
+        s5=V((32, 4, 8, 128), f32), r5=f_all, zr=V((8, 32, 256), f32), zi=V((8, 32, 256), f32), s6=block,
         kr=V((512, 128), f32), ki=V((512, 128), f32),
     )
     blocks, picked = pl.pallas_call(

time: 61.7 us -> 64.6 us (1.047)
  Pallas kernels: 60.5 us -> 63 us
    pallas_call x1, Pallas kernels: 58.7 us -> 61.2 us  [local(): pl.pallas_call(body, out_shape=(jax.ShapeDtypeStruct((8, 2, 32, 256), bf1...]
where the time goes in v4:
time: 64.6 us; the launch traced here: 63.6 us
  Pallas kernels  63 us (98%)
    pallas_call x1, Pallas kernels, local(): pl.pallas_call(body, out_shape=(jax.ShapeDtypeStruct((8, 2, 32, 256), bf1...  61.2 us
    pallas_call x1, Pallas kernels, local(): pl.pallas_call(finish, out_shape=(jax.ShapeDtypeStruct((2, 256, 256), f32...  1.78 us

profile of v4, /device:TPU:1, one launch (start us, length us, event | category | flops | bytes accessed | tf_op | source)
XLA Modules:
  0.0 63.6 jit_solution(10382278742094220918)
XLA Ops:
  0.6 61.2 %shard_map.158 = (bf16[8,2,32,256]{3,2,1,0:T(8,128)(2,1)}, f32[4,256]{1,0:T(4,128)}) custom-call(f32[2,256,256]{2,1,0:T(8,128)} %field.1, f32[2,2,256]{2,1,0:T(2,128)} %target.1, f32[2,8,1,256]{3,2,1,0:T(1,128)} %constant.26.clone.refs_0_, bf16[256,512]{1,0:T(8,128)(2,1)} %constant.27.clone.refs_1_, bf16[4,256,128]{2,1,0:T(8,128)(2,1)} %constant.28.clone.refs_2_, ...), custom_call_target="tpu_custom_call" | custom-call | tf_op jit(solution)/shard_map/pallas_call | solution.py:456
  61.9 1.8 %shard_map.159 = (f32[2,256,256]{2,1,0:T(8,128)}, f32[2,2,256]{2,1,0:T(2,128)}) custom-call(bf16[8,2,32,256]{3,2,1,0:T(8,128)(2,1)} %get-tuple-element.4.blocks, f32[4,256]{1,0:T(4,128)} %get-tuple-element.5.picked), custom_call_target="tpu_custom_call" | custom-call | tf_op jit(solution)/shard_map/pallas_call | solution.py:466

commit v5 on v3

--- a/solution.py
+++ b/solution.py
@@ -136,7 +136,7 @@
 
 FAR_FIRST = sorted(
     ((a, b) for a in range(8) for b in range(4)),
-    key=lambda p: -(min(p[0] >> 1, 4 - (p[0] >> 1)) + 2 * (p[0] & 1) + min(p[1], 4 - p[1])),
+    key=lambda p: (-min(p[0] >> 1, 4 - (p[0] >> 1)), -2 * (p[0] & 1) - min(p[1], 4 - p[1])),
 )
 QUARTERS = (2, 3, 1, 0)
 STEP = 8
@@ -413,10 +413,13 @@
             c, s = turn_row(T["tw"], 2 * q + v)
             zr[2 * q + v] = re * c - im * s
             zi[2 * q + v] = im * c + re * s
-    for c, (re, im) in enumerate(fft_list([(zr[v], zi[v]) for v in range(8)], 1)):
-        s6[c, 0] = re.astype(bf16)
-        s6[c, 1] = im.astype(bf16)
-    send_cols(lambda d: s6.at[d], r6, 7, 19)
+    blocks = fft_list([(zr[v], zi[v]) for v in range(8)], 1)
+    for half in range(2):
+        for c in range(8):
+            s6[c, half] = blocks[c][half].astype(bf16)
+        for k in (4, 1, 5, 3, 6, 2, 7):
+            d = ((col ^ k) & 4) + ((col + k) & 3)
+            copy_to(s6.at[d, half], r6.at[col, half], 7, 19, (row, d)).start()
     own = pltpu.make_async_copy(s6.at[col], r6.at[col], tsem.at[0])
     own.start()
     for slot, (src, count) in enumerate(((x1, 7), (tr, 7), (r2, 127), (r3, 127), (r4, 127), (ls, 7), (r5, 127), (s6, 7))):

time: 61.7 us -> 61.4 us (level)
  no operation moved by 1% of the time
where the time goes in v5:
time: 61.4 us; the launch traced here: 61.2 us
  Pallas kernels  60.6 us (99%)
  between operations  0.64 us (1%)
    pallas_call x1, Pallas kernels, local(): pl.pallas_call(body, out_shape=(jax.ShapeDtypeStruct((8, 2, 32, 256), bf1...  58.8 us
    pallas_call x1, Pallas kernels, local(): pl.pallas_call(finish, out_shape=(jax.ShapeDtypeStruct((2, 256, 256), f32...  1.78 us

profile of v5, /device:TPU:1, one launch (start us, length us, event | category | flops | bytes accessed | tf_op | source)
XLA Modules:
  0.0 61.2 jit_solution(13047950386752557654)
XLA Ops:
  0.6 58.8 %shard_map.158 = (bf16[8,2,32,256]{3,2,1,0:T(8,128)(2,1)}, f32[4,256]{1,0:T(4,128)}) custom-call(f32[2,256,256]{2,1,0:T(8,128)} %field.1, f32[2,2,256]{2,1,0:T(2,128)} %target.1, f32[2,8,1,256]{3,2,1,0:T(1,128)} %constant.26.clone.refs_0_, bf16[256,512]{1,0:T(8,128)(2,1)} %constant.27.clone.refs_1_, bf16[4,256,128]{2,1,0:T(8,128)(2,1)} %constant.28.clone.refs_2_, ...), custom_call_target="tpu_custom_call" | custom-call | tf_op jit(solution)/shard_map/pallas_call | solution.py:459
  59.4 1.8 %shard_map.159 = (f32[2,256,256]{2,1,0:T(8,128)}, f32[2,2,256]{2,1,0:T(2,128)}) custom-call(bf16[8,2,32,256]{3,2,1,0:T(8,128)(2,1)} %get-tuple-element.4.blocks, f32[4,256]{1,0:T(4,128)} %get-tuple-element.5.picked), custom_call_target="tpu_custom_call" | custom-call | tf_op jit(solution)/shard_map/pallas_call | solution.py:469
